TPU v7x, 256 devices: a whole 4x4x8 slice. The times are simulated.
256 devices in a mesh: space: 32 (over z_lo, y, core), fac: 8 (over z_hi, x).
Axes of the slice: x: 4, y: 4, z: 8 (z_hi: 2, z_lo: 4; z = z_hi * 4 + z_lo), core: 2. Of those that a mesh axis runs over, the one named last changes fastest.
Arguments:
- activations: bfloat16 [8, 64, 16, 16, 128], P('fac', 'space'), may hold values from -60 to 60
- out_grad: bfloat16 [8, 64, 16, 16, 128], P('fac', 'space'), may hold values from -60 to 60
- kernel: bfloat16 [27, 128, 128], replicated, may hold values from -0.109375 to 0.109375
Outputs:
- in_grad: bfloat16 [8, 64, 16, 16, 128], P('fac', 'space')
- update: float32 [27, 128, 128], P(None, 'fac')
All inputs are finite; a program needn't handle non-finite values.
Results may differ from a plain program's by a relative error of at most 0.0014.
Values may be sent and summed in bfloat16 or wider, within the bound.
No kernel may reach another device: no remote copies, remote signals or barrier semaphores. Data moves between devices by JAX's collectives and lax.ppermute only.
A program may use at most 128 MiB of HBM per device.

v0:
```python
import functools
import math

import jax
import jax.numpy as jnp
from jax import lax
from jax.experimental import pallas as pl
from jax.experimental.pallas import tpu as pltpu
from jax.sharding import PartitionSpec as P

damping = 0.1
clip_rate = 0.05
TAPS = 27
F32 = jnp.float32
BF16 = jnp.bfloat16
HI = lax.Precision.HIGHEST
VMEM = pl.BlockSpec(memory_space=pltpu.VMEM)
PARAMS = pltpu.CompilerParams(vmem_limit_bytes=48 * 1024 * 1024)

ORDER = 432
EDGES = (0, 128, 256, 384)
STARTS = (0, 432, 736, 912)
GRAD_AT = 960
COT_AT = 1392
PACKED = 1536
HALF = PACKED // 2
QUARTER = HALF // 4


SMEM = pl.BlockSpec(memory_space=pltpu.SMEM)
ANY = pl.BlockSpec(memory_space=pl.ANY)


def call(body, out_shape, scratch=(), name=None, spec=VMEM):
    def run(*args):
        return pl.pallas_call(
            body,
            out_shape=out_shape,
            in_specs=[SMEM if a.dtype == jnp.int32 else spec for a in args],
            out_specs=jax.tree.map(lambda _: VMEM, out_shape),
            scratch_shapes=list(scratch),
            compiler_params=PARAMS,
            name=name,
        )(*args)

    return run


def nt(a, b, precision=None):
    return lax.dot_general(a, b, (((1,), (1,)), ((), ())), precision=precision, preferred_element_type=F32)


def nn(a, b, precision=None):
    return lax.dot_general(a, b, (((1,), (0,)), ((), ())), precision=precision, preferred_element_type=F32)


def tn(a, b, precision=None):
    return lax.dot_general(a, b, (((0,), (0,)), ((), ())), precision=precision, preferred_element_type=F32)


def prep_kernel(place_ref, act_any, cot_any, give_ref, *rest):
    sends, (act_ref, cot_ref, act_t, sems) = rest[:4], rest[4:]
    copies = [
        pltpu.make_async_copy(act_any, act_ref, sems.at[0]),
        pltpu.make_async_copy(cot_any, cot_ref, sems.at[1]),
    ]
    for copy in copies:
        copy.start()
    for copy in copies:
        copy.wait()
    half = act_ref.shape[1] // 2
    act_t[...] = act_ref[...].astype(F32).T.astype(BF16)
    cot = cot_ref[...].astype(F32).T.astype(BF16)
    high, turn = place_ref[2], place_ref[3]
    give_ref[half:, :] = cot
    for k, send_ref in enumerate(sends):
        block = ((turn + k) % 4) * 16
        give_ref[16 * k : 16 * k + 16, :] = act_t[pl.ds(pl.multiple_of((1 - high) * half + block, 16), 16), :]
        send_ref[0:16, :] = act_t[pl.ds(pl.multiple_of(high * half + block, 16), 16), :]
        send_ref[16:, :] = cot


def spread_kernel(got_ref, *sends):
    for k, send_ref in enumerate(sends):
        send_ref[0:16, :] = got_ref[16 * k : 16 * k + 16, :]
        send_ref[16:, :] = got_ref[16 * len(sends) :, :]


def rim_kernel(*refs):
    parts, (first_ref, last_ref) = refs[:-2], refs[-2:]
    for s, ref in enumerate(parts):
        first_ref[16 * s : 16 * s + 16, :] = ref[0:16, 0:256]
        last_ref[16 * s : 16 * s + 16, :] = ref[0:16, 256:]
    first_ref[128:, :] = parts[0][16:, 0:256]
    last_ref[128:, :] = parts[0][16:, 256:]


def in_grad_kernel(prev_ref, cot_ref, next_ref, kern_ref, out_ref, rows_ref, shift_ref):
    rows_ref[8:264, :] = prev_ref[128:, :].astype(F32).T
    rows_ref[264:776, :] = cot_ref[...].astype(F32)
    rows_ref[776:1032, :] = next_ref[128:, :].astype(F32).T
    z = lax.broadcasted_iota(jnp.int32, (256, 128), 0) % 16
    zeros = jnp.zeros((16, 384), BF16)
    for plane in range(4):
        base = plane * 288
        shift_ref[base : base + 16, :] = zeros
        shift_ref[base + 272 : base + 288, :] = zeros
        for n, c in enumerate((-1, 0, 1)):
            at = 8 + plane * 256 + c
            cells = rows_ref[at : at + 256, :]
            if c:
                cells = jnp.where((z + c >= 0) & (z + c < 16), cells, 0.0)
            shift_ref[base + 16 : base + 272, n * 128 : (n + 1) * 128] = cells.astype(BF16)
    for x in range(2):
        total = jnp.zeros((256, 128), F32)
        for a in (-1, 0, 1):
            for b in (-1, 0, 1):
                for n, c in enumerate((-1, 0, 1)):
                    tap = 9 * (1 - a) + 3 * (1 - b) + (1 - c)
                    at = (x + 1 + a) * 288 + 16 + 16 * b
                    rows = shift_ref[at : at + 256, n * 128 : (n + 1) * 128]
                    total = total + nt(rows, kern_ref[tap])
        out_ref[x * 256 : (x + 1) * 256, :] = total.astype(BF16)


def stats_kernel(place_ref, prev_ref, next_ref, *refs, slabs):
    parts, (keep_ref, give_ref, x_ref, out_ref) = refs[:slabs], refs[slabs:]
    core, turn = place_ref[0], place_ref[1]
    lane = lax.broadcasted_iota(jnp.int32, (16, 1024), 1)
    y = (lane // 16) % 16
    z = lane % 16
    for s in range(slabs):
        cols = slice(s * 512, (s + 1) * 512)
        rim = slice(16 * s, 16 * s + 16)
        planes = jnp.concatenate([prev_ref[rim, :], parts[s][0:16, :], next_ref[rim, :]], axis=1).astype(F32)
        for b in (-1, 0, 1):
            for c in (-1, 0, 1):
                d = 16 * b + c
                moved = planes
                if d:
                    moved = pltpu.roll(planes, (-d) % 1024, 1)
                    ok = (y + b >= 0) & (y + b < 16) & (z + c >= 0) & (z + c < 16)
                    moved = jnp.where(ok, moved, 0.0)
                moved = moved.astype(BF16)
                for a in (-1, 0, 1):
                    tap = 9 * (a + 1) + 3 * (b + 1) + (c + 1)
                    at = (1 + a) * 256
                    x_ref[tap * 16 : (tap + 1) * 16, cols] = moved[:, at : at + 512]
        x_ref[ORDER:, cols] = parts[s][16:, :]
    for edge, start in zip(EDGES, STARTS):
        tile = nt(x_ref[edge:ORDER, :], x_ref[edge : edge + 128, :])
        out_ref[start : start + ORDER - edge, :] = tile
    out_ref[GRAD_AT : GRAD_AT + ORDER + 128, :] = nt(x_ref[...], x_ref[ORDER:, :])
    out_ref[COT_AT + 128 :, :] = jnp.zeros((PACKED - COT_AT - 128, 128), F32)
    for k in range(4):
        for half, ref in ((core, keep_ref), (1 - core, give_ref)):
            at = half * HALF + ((turn + k) % 4) * QUARTER
            ref[k * QUARTER : (k + 1) * QUARTER, :] = out_ref[pl.ds(pl.multiple_of(at, QUARTER), QUARTER), :]


def pair_kernel(keep_ref, got_ref, *outs):
    for k, out_ref in enumerate(outs):
        rows = slice(k * QUARTER, (k + 1) * QUARTER)
        out_ref[...] = keep_ref[rows, :] + got_ref[rows, :]


def fold_kernel(*refs):
    total = refs[0][...]
    for ref in refs[1:-1]:
        total = total + ref[...]
    refs[-1][...] = total


def fold_ring_kernel(a_ref, b_ref, c_ref, d_ref, out_ref):
    out_ref[...] = (a_ref[...] + c_ref[...]) + (b_ref[...] + d_ref[...])


def scale_kernel(raw_ref, parts_ref, out_ref, *, size):
    total = parts_ref[0]
    for p in range(1, parts_ref.shape[0]):
        total = total + parts_ref[p]
    factor = jnp.sqrt(clip_rate * size / total)[0:1, :]
    out_ref[...] = raw_ref[...] * factor


def spread(row):
    return jnp.broadcast_to(row, (8, 128))


def sweep(tiles, g, cols):
    shape = tiles[g].shape
    lane = lax.broadcasted_iota(jnp.int32, shape, 1) - 8 * g
    sub = lax.broadcasted_iota(jnp.int32, shape, 0)
    rows = tiles[g]

    def column(tile, at):
        return jnp.broadcast_to(tile[:, at : at + 1], shape)

    def row(tile, q):
        return jnp.broadcast_to(tile[q : q + 1, :], shape)

    def add(terms):
        while len(terms) > 1:
            terms = [x + y for x, y in zip(terms[::2], terms[1::2])]
        return terms[0]

    cols = [column(rows, 8 * g + q) for q in range(8)] if cols is None else list(cols)
    more = g + 1 < len(tiles)
    if more:
        block = [column(tiles[g + 1], 8 * g + 8 + q) for q in range(8)]
        beside = [column(tiles[g + 1], 8 * g + q) for q in range(8)]
    for k in range(0, 8, 2):
        one, two = cols[k], cols[k + 1]
        a, b, d = row(one, k), row(one, k + 1), row(two, k + 1)
        scale = 1.0 / (a * d - b * b)
        ia, ib, id_ = d * scale, -b * scale, a * scale
        upper, lower = sub == k, sub == k + 1
        for q in range(8):
            if q in (k, k + 1):
                continue
            h, l = row(cols[q], k), row(cols[q], k + 1)
            th, tl = ia * h + ib * l, ib * h + id_ * l
            cols[q] = jnp.where(upper, th, jnp.where(lower, tl, cols[q] - (one * th + two * tl)))
        cols[k] = jnp.where(upper, ia, jnp.where(lower, ib, -(one * ia + two * ib)))
        cols[k + 1] = jnp.where(upper, ib, jnp.where(lower, id_, -(one * ib + two * id_)))
    ahead = None
    if more:
        ahead = []
        for q in range(8):
            t = add([cols[r] * row(beside[r], q) for r in range(8)])
            ahead.append(block[q] - add([beside[r] * row(t, r) for r in range(8)]))
    swept = add([cols[q] * row(rows, q) for q in range(8)])
    for q in range(8):
        swept = jnp.where(lane == q, -cols[q], swept)
    heads = [row(swept, q) for q in range(8)]
    inside = (lane >= 0) & (lane < 8)
    out = list(tiles)
    for i in range(g + 1, len(tiles)):
        old = tiles[i]
        heavy = beside if i == g + 1 else [column(old, 8 * g + q) for q in range(8)]
        out[i] = jnp.where(inside, 0.0, old) - add([c * h for c, h in zip(heavy, heads)])
    p = jnp.where(lane < 0, rows, jnp.where(lane == sub, -1.0, 0.0))
    s = jnp.where(lane < 8, swept, 0.0)
    return out, p, s, ahead


class Factor:
    def __init__(self, mat):
        self.tiles = [mat[8 * i : 8 * i + 8] for i in range(mat.shape[0] // 8)]
        self.left, self.right, self.cols = [], [], None

    def step(self):
        self.tiles, p, s, self.cols = sweep(self.tiles, len(self.left), self.cols)
        self.left.append(p)
        self.right.append(s)

    def parts(self):
        return jnp.concatenate(self.left, axis=0), jnp.concatenate(self.right, axis=0)


def factor(mat, beside):
    out = Factor(mat)
    for _ in out.tiles:
        out.step()
        if beside:
            beside.pop(0)()
    while beside:
        beside.pop(0)()
    return out.parts()


def packed(tile, row, rows):
    at = STARTS[tile] + row - EDGES[tile]
    return slice(at, at + rows)


def forward_kernel(place_ref, *refs, count):
    mine, others = refs[:4], refs[4:8]
    z_ref, y_ref, right_ref, part_ref, stat_ref, b_ref = refs[8:]
    core, turn = place_ref[0], place_ref[1]
    for k in range(4):
        for half, ref in ((core, mine[k]), (1 - core, others[k])):
            at = half * HALF + ((turn + 4 - k) % 4) * QUARTER
            stat_ref[pl.ds(pl.multiple_of(at, QUARTER), QUARTER), :] = ref[...]
    eye = (
        lax.broadcasted_iota(jnp.int32, (128, 128), 0) == lax.broadcasted_iota(jnp.int32, (128, 128), 1)
    ).astype(F32)
    for t, edge in enumerate(EDGES):
        head = min(128, ORDER - edge)
        rows = stat_ref[packed(t, edge, ORDER - edge), :] / count
        y_ref[packed(t, edge, ORDER - edge), :] = rows
        y_ref[packed(t, edge, head), :] = rows[:head] + damping * eye[:head]
    b_ref[...] = stat_ref[GRAD_AT : GRAD_AT + ORDER, :] / math.sqrt(count)

    right = Factor(stat_ref[COT_AT : COT_AT + 128, :] / count + damping * eye)
    held = {}

    def idle():
        pass

    def finish_right():
        p, s = right.parts()
        right_ref[...] = tn(p, s, HI)

    beside = [right.step, idle] * 8
    d = y_ref[packed(0, 0, 128), :]
    for t, edge in enumerate(EDGES):
        size = min(128, ORDER - edge)
        below = edge + size
        left = ORDER - below
        if t == 1:
            work = beside
            beside = []
            for n in range(8):
                beside += work[n : n + 1] + [right.step]
            beside.append(finish_right)
        p, s = factor(d, beside)
        now = b_ref[edge:below, :]
        if left == 0:
            z = tn(p, nn(s, now, HI), HI)
            z_ref[edge:, :] = z
            held["sum"] = held["sum"] + tn(now, z, HI)
            break
        low = y_ref[packed(t, below, left), :]
        near = min(128, left)
        u_near, v_near = nt(low[:near], p, HI), nt(low[:near], s, HI)
        d = y_ref[packed(t + 1, below, near), 0:near] - nt(u_near, v_near, HI)

        def widen(low=low, p=p, s=s, u_near=u_near, v_near=v_near, near=near, left=left):
            held["u"], held["v"] = u_near, v_near
            if left > near:
                held["u"] = jnp.concatenate([u_near, nt(low[near:], p, HI)], axis=0)
                held["v"] = jnp.concatenate([v_near, nt(low[near:], s, HI)], axis=0)

        def into_tile(tile, low=low, below=below, near=near):
            first = max(EDGES[tile] - below, near)
            if first >= low.shape[0]:
                return
            at = EDGES[tile] - below
            wide = min(128, ORDER - EDGES[tile])
            span = packed(tile, below + first, low.shape[0] - first)
            y_ref[span, 0:wide] = y_ref[span, 0:wide] - nt(held["u"][first:], held["v"][at : at + wide], HI)

        def into_rhs(p=p, s=s, now=now, t=t, edge=edge, below=below, left=left):
            half = nn(s, now, HI)
            z = tn(p, half, HI)
            z_ref[edge:below, :] = z
            b_ref[below:, :] = b_ref[below:, :] - nn(held["u"], half, HI)
            term = tn(now, z, HI)
            held["sum"] = held["sum"] + term if t else term

        def scale_rows(s=s, t=t, below=below, left=left):
            y_ref[packed(t, below, left), :] = nn(held["u"], s, HI)

        beside = [widen] + [functools.partial(into_tile, r) for r in range(t + 1, len(EDGES))]
        beside += [into_rhs, scale_rows]
    prod = held["sum"] * right_ref[...]
    acc = prod[0:8]
    for i in range(1, 16):
        acc = acc + prod[8 * i : 8 * i + 8]
    part_ref[...] = jnp.broadcast_to(jnp.sum(acc).reshape(1, 1, 1), part_ref.shape)


def backward_kernel(z_ref, y_ref, right_ref, raw_ref, x_ref):
    for t in reversed(range(len(EDGES))):
        below = min(EDGES[t] + 128, ORDER)
        x = z_ref[EDGES[t] : below, :]
        if below < ORDER:
            x = x - tn(y_ref[packed(t, below, ORDER - below), :], x_ref[below:, :], HI)
        x_ref[EDGES[t] : below, :] = x
    raw_ref[...] = nn(x_ref[...], right_ref[...], HI)


def on_device(activations, out_grad, kernel):
    shape = activations.shape
    spaces = lax.axis_size("space")
    groups = lax.axis_size("fac")
    wide = groups // 2
    act = activations.reshape(512, 128)
    cot = out_grad.reshape(512, 128)

    sp, fa = lax.axis_index("space"), lax.axis_index("fac")
    place = jnp.stack([sp % 2, sp // 2 % 4, fa // wide, fa % wide]).astype(jnp.int32)
    up = [(i, i + 1) for i in range(spaces - 1)]
    down = [(i + 1, i) for i in range(spaces - 1)]
    swap = [(i, i ^ 1) for i in range(spaces)]
    ends = [(i, (i + wide) % groups) for i in range(groups)]

    def ring_x(k):
        return [(i, i // wide * wide + (i + k) % wide) for i in range(groups)]

    def ring_y(k):
        return [(i, i // 8 * 8 + (i // 2 % 4 + k) % 4 * 2 + i % 2) for i in range(spaces)]

    def ring_z(k):
        return [(i, (i // 8 + k) % 4 * 8 + i % 8) for i in range(spaces)]

    def rows(count, width=128, dtype=F32):
        return jax.ShapeDtypeStruct((count, width), dtype)

    part = rows(144, 512, BF16)
    give, *sends = call(
        prep_kernel,
        (rows(192, 512, BF16),) + (part,) * 4,
        scratch=[pltpu.VMEM((512, 128), BF16)] * 2 + [pltpu.VMEM((128, 512), BF16), pltpu.SemaphoreType.DMA((2,))],
        name="prep",
        spec=ANY,
    )(place, act, cot)
    got = lax.ppermute(give, "fac", ends)
    own = [sends[0]] + [lax.ppermute(sends[k], "fac", ring_x(k)) for k in (1, 2, 3)]
    got, own = lax.optimization_barrier((got, own))

    sends = call(spread_kernel, (part,) * 4, name="spread")(got)
    far = [sends[0]] + [lax.ppermute(sends[k], "fac", ring_x(k)) for k in (1, 2, 3)]
    parts = own + far

    first, last = call(rim_kernel, (rows(256, 256, BF16),) * 2, name="rim")(*parts)
    prev = lax.ppermute(last, "space", up)
    following = lax.ppermute(first, "space", down)

    keep, give = call(
        functools.partial(stats_kernel, slabs=groups),
        (rows(HALF),) * 2,
        scratch=[pltpu.VMEM((ORDER + 128, groups * 512), BF16), pltpu.VMEM((PACKED, 128), F32)],
        name="stats",
    )(place, prev, following, *parts)
    in_grad = call(
        in_grad_kernel,
        rows(512, 128, BF16),
        scratch=[pltpu.VMEM((1040, 128), F32), pltpu.VMEM((1152, 384), BF16)],
        name="in_grad",
    )(prev, cot, following, kernel)

    got = lax.ppermute(give, "space", swap)
    quarters = call(pair_kernel, (rows(QUARTER),) * 4, name="pair")(keep, got)
    over_y = [lax.ppermute(quarters[k], "space", ring_y(k)) for k in (1, 2, 3)]
    over_y, in_grad = lax.optimization_barrier((over_y, in_grad))
    mine = call(fold_kernel, rows(QUARTER), name="fold_y")(quarters[0], *over_y)
    over_z = [lax.ppermute(mine, "space", ring_z(k)) for k in (1, 2, 3)]
    mine = call(fold_ring_kernel, rows(QUARTER), name="fold_z")(mine, *over_z)
    mine = [mine] + [lax.ppermute(mine, "space", ring_y(k)) for k in (1, 2, 3)]
    others = [lax.ppermute(q, "space", swap) for q in mine]

    z, y, right, total = call(
        functools.partial(forward_kernel, count=float(512 * spaces * groups)),
        (rows(ORDER), rows(GRAD_AT), rows(128), jax.ShapeDtypeStruct((groups, 8, 128), F32)),
        scratch=[pltpu.VMEM((PACKED, 128), F32), pltpu.VMEM((ORDER, 128), F32)],
        name="forward",
    )(place, *mine, *others)
    every = lax.all_to_all(total, "fac", 0, 0, tiled=True)
    raw = call(backward_kernel, rows(ORDER), scratch=[pltpu.VMEM((ORDER, 128), F32)], name="backward")(z, y, right)
    update = call(functools.partial(scale_kernel, size=kernel.size), rows(ORDER), name="scale")(raw, every)
    return (in_grad.reshape(shape), update.reshape(TAPS, 16, 128))


def solution(mesh):
    placed = (P("fac", "space", None, None, None), P("fac", "space", None, None, None), P())
    return jax.shard_map(
        on_device,
        mesh=mesh,
        in_specs=placed,
        out_specs=(P("fac", "space", None, None, None), P(None, "fac", None)),
        check_vma=False,
    )
```

profile of v0, /device:TPU:1, one launch (start us, length us, event | category | flops | bytes accessed | tf_op | source)
XLA Modules:
  0.0 119.4 jit_solution(13723703126918546544)
XLA Ops:
  3.6 7.8 %collective-permute-start = (bf16[192,512]{1,0:T(8,128)(2,1)S(1)}, bf16[192,512]{1,0:T(8,128)(2,1)S(1)}, u32[]{:S(2)}, u32[]{:S(2)}) collective-permute-start(bf16[192,512]{1,0:T(8,128)(2,1)S(1)} %get-tuple-element.32), channel_id=1, source_target_pairs={{0,4},{1,5},{2,6},{3,7},{4,0},{5,1},{6,2},{7,3},{8,12},{9,13},{10,... | collective-permute-start | bytes 589832 | tf_op jit(solution)/shard_map/ppermute | solution.py:409
  12.7 2.5 %collective-permute-start.2 = (bf16[144,512]{1,0:T(8,128)(2,1)S(1)}, bf16[144,512]{1,0:T(8,128)(2,1)S(1)}, u32[]{:S(2)}, u32[]{:S(2)}) collective-permute-start(bf16[144,512]{1,0:T(8,128)(2,1)S(1)} %get-tuple-element.35), channel_id=1, source_target_pairs={{0,2},{1,3},{2,0},{3,1},{4,6},{5,7},{6,4},{7,5},{8,10},{9,11},{10,... | collective-permute-start | bytes 442376 | tf_op jit(solution)/shard_map/ppermute | solution.py:410
  17.1 4.1 %collective-permute-done.2.refs_2_ = bf16[144,512]{1,0:T(8,128)(2,1)S(1)} collective-permute-done((bf16[144,512]{1,0:T(8,128)(2,1)S(1)}, bf16[144,512]{1,0:T(8,128)(2,1)S(1)}, u32[]{:S(2)}, u32[]{:S(2)}) %collective-permute-start.2) | collective-permute-done | bytes 147488 | tf_op jit(solution)/shard_map/ppermute | solution.py:410
  21.3 1.8 %collective-permute-start.4 = (bf16[144,512]{1,0:T(8,128)(2,1)S(1)}, bf16[144,512]{1,0:T(8,128)(2,1)S(1)}, u32[]{:S(2)}, u32[]{:S(2)}) collective-permute-start(bf16[144,512]{1,0:T(8,128)(2,1)S(1)} %get-tuple-element.43), channel_id=1, source_target_pairs={{0,1},{1,2},{2,3},{3,0},{4,5},{5,6},{6,7},{7,4},{8,9},{9,10},{10,1... | collective-permute-start | bytes 442376 | tf_op jit(solution)/shard_map/ppermute | solution.py:414
  23.0 2.0 %collective-permute-start.5 = (bf16[144,512]{1,0:T(8,128)(2,1)S(1)}, bf16[144,512]{1,0:T(8,128)(2,1)S(1)}, u32[]{:S(2)}, u32[]{:S(2)}) collective-permute-start(bf16[144,512]{1,0:T(8,128)(2,1)S(1)} %get-tuple-element.44), channel_id=1, source_target_pairs={{0,2},{1,3},{2,0},{3,1},{4,6},{5,7},{6,4},{7,5},{8,10},{9,11},{10,... | collective-permute-start | bytes 442376 | tf_op jit(solution)/shard_map/ppermute | solution.py:414
  26.5 3.8 %collective-permute-done.5.refs_6_ = bf16[144,512]{1,0:T(8,128)(2,1)S(1)} collective-permute-done((bf16[144,512]{1,0:T(8,128)(2,1)S(1)}, bf16[144,512]{1,0:T(8,128)(2,1)S(1)}, u32[]{:S(2)}, u32[]{:S(2)}) %collective-permute-start.5) | collective-permute-done | bytes 147488 | tf_op jit(solution)/shard_map/ppermute | solution.py:414
  30.4 5.7 %collective-permute-start.7 = (bf16[256,256]{1,0:T(8,128)(2,1)S(1)}, bf16[256,256]{1,0:T(8,128)(2,1)S(1)}, u32[]{:S(2)}, u32[]{:S(2)}) collective-permute-start(bf16[256,256]{1,0:T(8,128)(2,1)S(1)} %get-tuple-element.46), channel_id=1, source_target_pairs={{0,8},{8,16},{16,24},{24,32},{32,40},{40,48},{48,56},{56,64},{64,7... | collective-permute-start | bytes 393224 | tf_op jit(solution)/shard_map/ppermute | solution.py:418
  36.1 2.1 %collective-permute-start.8 = (bf16[256,256]{1,0:T(8,128)(2,1)S(1)}, bf16[256,256]{1,0:T(8,128)(2,1)S(1)}, u32[]{:S(2)}, u32[]{:S(2)}) collective-permute-start(bf16[256,256]{1,0:T(8,128)(2,1)S(1)} %get-tuple-element.47), channel_id=1, source_target_pairs={{8,0},{16,8},{24,16},{32,24},{40,32},{48,40},{56,48},{64,56},{72,6... | collective-permute-start | bytes 393224 | tf_op jit(solution)/shard_map/ppermute | solution.py:419
  38.2 4.3 %collective-permute-done.8.next_ref = bf16[256,256]{1,0:T(8,128)(2,1)S(1)} collective-permute-done((bf16[256,256]{1,0:T(8,128)(2,1)S(1)}, bf16[256,256]{1,0:T(8,128)(2,1)S(1)}, u32[]{:S(2)}, u32[]{:S(2)}) %collective-permute-start.8) | collective-permute-done | bytes 131104 | tf_op jit(solution)/shard_map/ppermute | solution.py:419
  42.6 4.3 %stats.1 = (f32[768,128]{1,0:T(8,128)S(1)}, f32[768,128]{1,0:T(8,128)S(1)}) custom-call(s32[4]{0:T(128)S(1)} %pad_add_fusion.place_ref, bf16[256,256]{1,0:T(8,128)(2,1)S(1)} %collective-permute-done.7.prev_ref, bf16[256,256]{1,0:T(8,128)(2,1)S(1)} %collective-permute-done.8.next_ref, bf16[144,512]{1,0:T(8,128)(2,1)S(1)} %get-tuple-element.37.refs_0_, ...), custom_call_target="tpu_custom_call" | custom-call | tf_op jit(solution)/shard_map/stats/pallas_call | solution.py:36
  46.9 1.7 %collective-permute-done.9.got_ref = f32[768,128]{1,0:T(8,128)S(1)} collective-permute-done((f32[768,128]{1,0:T(8,128)S(1)}, f32[768,128]{1,0:T(8,128)S(1)}, u32[]{:S(2)}, u32[]{:S(2)}) %collective-permute-start.9) | collective-permute-done | bytes 393248 | tf_op jit(solution)/shard_map/ppermute | solution.py:434
  48.7 1.4 %collective-permute-start.10 = (f32[192,128]{1,0:T(8,128)S(1)}, f32[192,128]{1,0:T(8,128)S(1)}, u32[]{:S(2)}, u32[]{:S(2)}) collective-permute-start(f32[192,128]{1,0:T(8,128)S(1)} %get-tuple-element.50), channel_id=1, source_target_pairs={{0,16},{8,24},{16,32},{24,40},{32,48},{40,56},{48,0},{56,8},{64,80... | collective-permute-start | bytes 294920 | tf_op jit(solution)/shard_map/ppermute | solution.py:436
  50.1 3.8 %collective-permute-start.11 = (f32[192,128]{1,0:T(8,128)S(1)}, f32[192,128]{1,0:T(8,128)S(1)}, u32[]{:S(2)}, u32[]{:S(2)}) collective-permute-start(f32[192,128]{1,0:T(8,128)S(1)} %get-tuple-element.51), channel_id=1, source_target_pairs={{0,32},{8,40},{16,48},{24,56},{32,0},{40,8},{48,16},{56,24},{64,96... | collective-permute-start | bytes 294920 | tf_op jit(solution)/shard_map/ppermute | solution.py:436
  53.9 1.9 %in_grad.1 = bf16[512,128]{1,0:T(8,128)(2,1)} custom-call(bf16[256,256]{1,0:T(8,128)(2,1)S(1)} %collective-permute-done.7.prev_ref, bf16[512,128]{1,0:T(8,128)(2,1)S(1)} %bitcast.9, bf16[256,256]{1,0:T(8,128)(2,1)S(1)} %collective-permute-done.8.next_ref, bf16[27,128,128]{2,1,0:T(8,128)(2,1)S(1)} %copy-done), custom_call_target="tpu_custom_call" | custom-call | tf_op jit(solution)/shard_map/in_grad/pallas_call | solution.py:36
  55.8 3.0 %collective-permute-done.11.refs_2_ = f32[192,128]{1,0:T(8,128)S(1)} collective-permute-done((f32[192,128]{1,0:T(8,128)S(1)}, f32[192,128]{1,0:T(8,128)S(1)}, u32[]{:S(2)}, u32[]{:S(2)}) %collective-permute-start.11) | collective-permute-done | bytes 98336 | tf_op jit(solution)/shard_map/ppermute | solution.py:436
  59.1 1.9 %collective-permute-start.14 = (f32[192,128]{1,0:T(8,128)S(1)}, f32[192,128]{1,0:T(8,128)S(1)}, u32[]{:S(2)}, u32[]{:S(2)}) collective-permute-start(f32[192,128]{1,0:T(8,128)S(1)} %fold_y.1.a_ref), channel_id=1, source_target_pairs={{0,128},{8,136},{16,144},{24,152},{32,160},{40,168},{48,176},{56,1... | collective-permute-start | bytes 294920 | tf_op jit(solution)/shard_map/ppermute | solution.py:439
  62.6 6.6 %collective-permute-done.14.c_ref = f32[192,128]{1,0:T(8,128)S(1)} collective-permute-done((f32[192,128]{1,0:T(8,128)S(1)}, f32[192,128]{1,0:T(8,128)S(1)}, u32[]{:S(2)}, u32[]{:S(2)}) %collective-permute-start.14) | collective-permute-done | bytes 98336 | tf_op jit(solution)/shard_map/ppermute | solution.py:439
  69.2 3.0 %collective-permute-start.18 = (f32[192,128]{1,0:T(8,128)S(1)}, f32[192,128]{1,0:T(8,128)S(1)}, u32[]{:S(2)}, u32[]{:S(2)}) collective-permute-start(f32[192,128]{1,0:T(8,128)S(1)} %fold_z.1.refs_0_), channel_id=1, source_target_pairs={{0,48},{8,56},{16,0},{24,8},{32,16},{40,24},{48,32},{56,40},{64,11... | collective-permute-start | bytes 294920 | tf_op jit(solution)/shard_map/ppermute | solution.py:441
  72.9 1.9 %collective-permute-start.19 = (f32[192,128]{1,0:T(8,128)S(1)}, f32[192,128]{1,0:T(8,128)S(1)}, u32[]{:S(2)}, u32[]{:S(2)}) collective-permute-start(f32[192,128]{1,0:T(8,128)S(1)} %fold_z.1.refs_0_), channel_id=1, source_target_pairs={{0,8},{8,0},{16,24},{24,16},{32,40},{40,32},{48,56},{56,48},{64,72... | collective-permute-start | bytes 294920 | tf_op jit(solution)/shard_map/ppermute | solution.py:442
  74.8 2.6 %collective-permute-start.22 = (f32[192,128]{1,0:T(8,128)S(1)}, f32[192,128]{1,0:T(8,128)S(1)}, u32[]{:S(2)}, u32[]{:S(2)}) collective-permute-start(f32[192,128]{1,0:T(8,128)S(1)} %collective-permute-done.18.refs_3_), channel_id=1, source_target_pairs={{0,8},{8,0},{16,24},{24,16},{32,40},{40,32},{48,56},{56,48},{64,72... | collective-permute-start | bytes 294920 | tf_op jit(solution)/shard_map/ppermute | solution.py:442
  77.4 2.7 %collective-permute-start.21 = (f32[192,128]{1,0:T(8,128)S(1)}, f32[192,128]{1,0:T(8,128)S(1)}, u32[]{:S(2)}, u32[]{:S(2)}) collective-permute-start(f32[192,128]{1,0:T(8,128)S(1)} %collective-permute-done.17.refs_2_), channel_id=1, source_target_pairs={{0,8},{8,0},{16,24},{24,16},{32,40},{40,32},{48,56},{56,48},{64,72... | collective-permute-start | bytes 294920 | tf_op jit(solution)/shard_map/ppermute | solution.py:442
  82.0 20.5 %forward.1 = (f32[432,128]{1,0:T(8,128)S(1)}, f32[960,128]{1,0:T(8,128)S(1)}, f32[128,128]{1,0:T(8,128)S(1)}, f32[8,8,128]{2,1,0:T(8,128)}) custom-call(s32[4]{0:T(128)S(1)} %pad_add_fusion.place_ref, f32[192,128]{1,0:T(8,128)S(1)} %fold_z.1.refs_0_, f32[192,128]{1,0:T(8,128)S(1)} %collective-permute-done.16.refs_1_, ...), custom_call_target="tpu_custom_call" | custom-call | tf_op jit(solution)/shard_map/forward/pallas_call | solution.py:36
  102.4 7.2 %all-to-all-start = ((f32[8,8,128]{2,1,0:T(8,128)}), f32[8,8,128]{2,1,0:T(8,128)S(1)}, u32[]{:S(2)}, u32[]{:S(2)}) async-start(f32[8,8,128]{2,1,0:T(8,128)} %get-tuple-element.61), calls=%async_computation | async-start | bytes 65536 | tf_op jit(solution)/shard_map/all_to_all | solution.py:450
  110.9 7.8 %all-to-all-done.parts_ref = f32[8,8,128]{2,1,0:T(8,128)S(1)} async-done(((f32[8,8,128]{2,1,0:T(8,128)}), f32[8,8,128]{2,1,0:T(8,128)S(1)}, u32[]{:S(2)}, u32[]{:S(2)}) %all-to-all-start) | async-done | bytes 32800 | tf_op jit(solution)/shard_map/all_to_all | solution.py:450
  (44 shorter events, 14.3 us)
Async XLA Ops:
  3.6 17.6 %collective-permute-start = (bf16[192,512]{1,0:T(8,128)(2,1)S(1)}, bf16[192,512]{1,0:T(8,128)(2,1)S(1)}, u32[]{:S(2)}, u32[]{:S(2)}) collective-permute-start(bf16[192,512]{1,0:T(8,128)(2,1)S(1)} %get-tuple-element.32), channel_id=1, source_target_pairs={{0,4},{1,5},{2,6},{3,7},{4,0},{5,1},{6,2},{7,3},{8,12},{9,13},{10,... | collective-permute-start | bytes 589832 | tf_op jit(solution)/shard_map/ppermute | solution.py:409
  11.5 5.6 %collective-permute-start.1 = (bf16[144,512]{1,0:T(8,128)(2,1)S(1)}, bf16[144,512]{1,0:T(8,128)(2,1)S(1)}, u32[]{:S(2)}, u32[]{:S(2)}) collective-permute-start(bf16[144,512]{1,0:T(8,128)(2,1)S(1)} %get-tuple-element.34), channel_id=1, source_target_pairs={{0,1},{1,2},{2,3},{3,0},{4,5},{5,6},{6,7},{7,4},{8,9},{9,10},{10,1... | collective-permute-start | bytes 442376 | tf_op jit(solution)/shard_map/ppermute | solution.py:410
  12.7 8.5 %collective-permute-start.2 = (bf16[144,512]{1,0:T(8,128)(2,1)S(1)}, bf16[144,512]{1,0:T(8,128)(2,1)S(1)}, u32[]{:S(2)}, u32[]{:S(2)}) collective-permute-start(bf16[144,512]{1,0:T(8,128)(2,1)S(1)} %get-tuple-element.35), channel_id=1, source_target_pairs={{0,2},{1,3},{2,0},{3,1},{4,6},{5,7},{6,4},{7,5},{8,10},{9,11},{10,... | collective-permute-start | bytes 442376 | tf_op jit(solution)/shard_map/ppermute | solution.py:410
  15.1 6.1 %collective-permute-start.3 = (bf16[144,512]{1,0:T(8,128)(2,1)S(1)}, bf16[144,512]{1,0:T(8,128)(2,1)S(1)}, u32[]{:S(2)}, u32[]{:S(2)}) collective-permute-start(bf16[144,512]{1,0:T(8,128)(2,1)S(1)} %get-tuple-element.36), channel_id=1, source_target_pairs={{0,3},{1,0},{2,1},{3,2},{4,7},{5,4},{6,5},{7,6},{8,11},{9,8},{10,9... | collective-permute-start | bytes 442376 | tf_op jit(solution)/shard_map/ppermute | solution.py:410
  21.3 5.3 %collective-permute-start.4 = (bf16[144,512]{1,0:T(8,128)(2,1)S(1)}, bf16[144,512]{1,0:T(8,128)(2,1)S(1)}, u32[]{:S(2)}, u32[]{:S(2)}) collective-permute-start(bf16[144,512]{1,0:T(8,128)(2,1)S(1)} %get-tuple-element.43), channel_id=1, source_target_pairs={{0,1},{1,2},{2,3},{3,0},{4,5},{5,6},{6,7},{7,4},{8,9},{9,10},{10,1... | collective-permute-start | bytes 442376 | tf_op jit(solution)/shard_map/ppermute | solution.py:414
  23.0 7.3 %collective-permute-start.5 = (bf16[144,512]{1,0:T(8,128)(2,1)S(1)}, bf16[144,512]{1,0:T(8,128)(2,1)S(1)}, u32[]{:S(2)}, u32[]{:S(2)}) collective-permute-start(bf16[144,512]{1,0:T(8,128)(2,1)S(1)} %get-tuple-element.44), channel_id=1, source_target_pairs={{0,2},{1,3},{2,0},{3,1},{4,6},{5,7},{6,4},{7,5},{8,10},{9,11},{10,... | collective-permute-start | bytes 442376 | tf_op jit(solution)/shard_map/ppermute | solution.py:414
  25.0 5.3 %collective-permute-start.6 = (bf16[144,512]{1,0:T(8,128)(2,1)S(1)}, bf16[144,512]{1,0:T(8,128)(2,1)S(1)}, u32[]{:S(2)}, u32[]{:S(2)}) collective-permute-start(bf16[144,512]{1,0:T(8,128)(2,1)S(1)} %get-tuple-element.45), channel_id=1, source_target_pairs={{0,3},{1,0},{2,1},{3,2},{4,7},{5,4},{6,5},{7,6},{8,11},{9,8},{10,9... | collective-permute-start | bytes 442376 | tf_op jit(solution)/shard_map/ppermute | solution.py:414
  30.4 7.8 %collective-permute-start.7 = (bf16[256,256]{1,0:T(8,128)(2,1)S(1)}, bf16[256,256]{1,0:T(8,128)(2,1)S(1)}, u32[]{:S(2)}, u32[]{:S(2)}) collective-permute-start(bf16[256,256]{1,0:T(8,128)(2,1)S(1)} %get-tuple-element.46), channel_id=1, source_target_pairs={{0,8},{8,16},{16,24},{24,32},{32,40},{40,48},{48,56},{56,64},{64,7... | collective-permute-start | bytes 393224 | tf_op jit(solution)/shard_map/ppermute | solution.py:418
  36.1 6.4 %collective-permute-start.8 = (bf16[256,256]{1,0:T(8,128)(2,1)S(1)}, bf16[256,256]{1,0:T(8,128)(2,1)S(1)}, u32[]{:S(2)}, u32[]{:S(2)}) collective-permute-start(bf16[256,256]{1,0:T(8,128)(2,1)S(1)} %get-tuple-element.47), channel_id=1, source_target_pairs={{8,0},{16,8},{24,16},{32,24},{40,32},{48,40},{56,48},{64,56},{72,6... | collective-permute-start | bytes 393224 | tf_op jit(solution)/shard_map/ppermute | solution.py:419
  46.8 1.8 %collective-permute-start.9 = (f32[768,128]{1,0:T(8,128)S(1)}, f32[768,128]{1,0:T(8,128)S(1)}, u32[]{:S(2)}, u32[]{:S(2)}) collective-permute-start(f32[768,128]{1,0:T(8,128)S(1)} %get-tuple-element.49), channel_id=1, source_target_pairs={{0,8},{8,0},{16,24},{24,16},{32,40},{40,32},{48,56},{56,48},{64,72... | collective-permute-start | bytes 1179656 | tf_op jit(solution)/shard_map/ppermute | solution.py:434
  48.7 7.1 %collective-permute-start.10 = (f32[192,128]{1,0:T(8,128)S(1)}, f32[192,128]{1,0:T(8,128)S(1)}, u32[]{:S(2)}, u32[]{:S(2)}) collective-permute-start(f32[192,128]{1,0:T(8,128)S(1)} %get-tuple-element.50), channel_id=1, source_target_pairs={{0,16},{8,24},{16,32},{24,40},{32,48},{40,56},{48,0},{56,8},{64,80... | collective-permute-start | bytes 294920 | tf_op jit(solution)/shard_map/ppermute | solution.py:436
  50.1 8.7 %collective-permute-start.11 = (f32[192,128]{1,0:T(8,128)S(1)}, f32[192,128]{1,0:T(8,128)S(1)}, u32[]{:S(2)}, u32[]{:S(2)}) collective-permute-start(f32[192,128]{1,0:T(8,128)S(1)} %get-tuple-element.51), channel_id=1, source_target_pairs={{0,32},{8,40},{16,48},{24,56},{32,0},{40,8},{48,16},{56,24},{64,96... | collective-permute-start | bytes 294920 | tf_op jit(solution)/shard_map/ppermute | solution.py:436
  53.9 4.9 %collective-permute-start.12 = (f32[192,128]{1,0:T(8,128)S(1)}, f32[192,128]{1,0:T(8,128)S(1)}, u32[]{:S(2)}, u32[]{:S(2)}) collective-permute-start(f32[192,128]{1,0:T(8,128)S(1)} %get-tuple-element.52), channel_id=1, source_target_pairs={{0,48},{8,56},{16,0},{24,8},{32,16},{40,24},{48,32},{56,40},{64,11... | collective-permute-start | bytes 294920 | tf_op jit(solution)/shard_map/ppermute | solution.py:436
  58.8 3.7 %collective-permute-start.15 = (f32[192,128]{1,0:T(8,128)S(1)}, f32[192,128]{1,0:T(8,128)S(1)}, u32[]{:S(2)}, u32[]{:S(2)}) collective-permute-start(f32[192,128]{1,0:T(8,128)S(1)} %fold_y.1.a_ref), channel_id=1, source_target_pairs={{0,192},{8,200},{16,208},{24,216},{32,224},{40,232},{48,240},{56,2... | collective-permute-start | bytes 294920 | tf_op jit(solution)/shard_map/ppermute | solution.py:439
  59.1 10.0 %collective-permute-start.14 = (f32[192,128]{1,0:T(8,128)S(1)}, f32[192,128]{1,0:T(8,128)S(1)}, u32[]{:S(2)}, u32[]{:S(2)}) collective-permute-start(f32[192,128]{1,0:T(8,128)S(1)} %fold_y.1.a_ref), channel_id=1, source_target_pairs={{0,128},{8,136},{16,144},{24,152},{32,160},{40,168},{48,176},{56,1... | collective-permute-start | bytes 294920 | tf_op jit(solution)/shard_map/ppermute | solution.py:439
  61.0 8.1 %collective-permute-start.13 = (f32[192,128]{1,0:T(8,128)S(1)}, f32[192,128]{1,0:T(8,128)S(1)}, u32[]{:S(2)}, u32[]{:S(2)}) collective-permute-start(f32[192,128]{1,0:T(8,128)S(1)} %fold_y.1.a_ref), channel_id=1, source_target_pairs={{0,64},{8,72},{16,80},{24,88},{32,96},{40,104},{48,112},{56,120},{... | collective-permute-start | bytes 294920 | tf_op jit(solution)/shard_map/ppermute | solution.py:439
  69.2 5.6 %collective-permute-start.18 = (f32[192,128]{1,0:T(8,128)S(1)}, f32[192,128]{1,0:T(8,128)S(1)}, u32[]{:S(2)}, u32[]{:S(2)}) collective-permute-start(f32[192,128]{1,0:T(8,128)S(1)} %fold_z.1.refs_0_), channel_id=1, source_target_pairs={{0,48},{8,56},{16,0},{24,8},{32,16},{40,24},{48,32},{56,40},{64,11... | collective-permute-start | bytes 294920 | tf_op jit(solution)/shard_map/ppermute | solution.py:441
  72.2 5.2 %collective-permute-start.17 = (f32[192,128]{1,0:T(8,128)S(1)}, f32[192,128]{1,0:T(8,128)S(1)}, u32[]{:S(2)}, u32[]{:S(2)}) collective-permute-start(f32[192,128]{1,0:T(8,128)S(1)} %fold_z.1.refs_0_), channel_id=1, source_target_pairs={{0,32},{8,40},{16,48},{24,56},{32,0},{40,8},{48,16},{56,24},{64,96... | collective-permute-start | bytes 294920 | tf_op jit(solution)/shard_map/ppermute | solution.py:441
  72.7 7.3 %collective-permute-start.16 = (f32[192,128]{1,0:T(8,128)S(1)}, f32[192,128]{1,0:T(8,128)S(1)}, u32[]{:S(2)}, u32[]{:S(2)}) collective-permute-start(f32[192,128]{1,0:T(8,128)S(1)} %fold_z.1.refs_0_), channel_id=1, source_target_pairs={{0,16},{8,24},{16,32},{24,40},{32,48},{40,56},{48,0},{56,8},{64,80... | collective-permute-start | bytes 294920 | tf_op jit(solution)/shard_map/ppermute | solution.py:441
  72.9 8.1 %collective-permute-start.19 = (f32[192,128]{1,0:T(8,128)S(1)}, f32[192,128]{1,0:T(8,128)S(1)}, u32[]{:S(2)}, u32[]{:S(2)}) collective-permute-start(f32[192,128]{1,0:T(8,128)S(1)} %fold_z.1.refs_0_), channel_id=1, source_target_pairs={{0,8},{8,0},{16,24},{24,16},{32,40},{40,32},{48,56},{56,48},{64,72... | collective-permute-start | bytes 294920 | tf_op jit(solution)/shard_map/ppermute | solution.py:442
  74.8 6.3 %collective-permute-start.22 = (f32[192,128]{1,0:T(8,128)S(1)}, f32[192,128]{1,0:T(8,128)S(1)}, u32[]{:S(2)}, u32[]{:S(2)}) collective-permute-start(f32[192,128]{1,0:T(8,128)S(1)} %collective-permute-done.18.refs_3_), channel_id=1, source_target_pairs={{0,8},{8,0},{16,24},{24,16},{32,40},{40,32},{48,56},{56,48},{64,72... | collective-permute-start | bytes 294920 | tf_op jit(solution)/shard_map/ppermute | solution.py:442
  77.4 3.7 %collective-permute-start.21 = (f32[192,128]{1,0:T(8,128)S(1)}, f32[192,128]{1,0:T(8,128)S(1)}, u32[]{:S(2)}, u32[]{:S(2)}) collective-permute-start(f32[192,128]{1,0:T(8,128)S(1)} %collective-permute-done.17.refs_2_), channel_id=1, source_target_pairs={{0,8},{8,0},{16,24},{24,16},{32,40},{40,32},{48,56},{56,48},{64,72... | collective-permute-start | bytes 294920 | tf_op jit(solution)/shard_map/ppermute | solution.py:442
  80.0 1.9 %collective-permute-start.20 = (f32[192,128]{1,0:T(8,128)S(1)}, f32[192,128]{1,0:T(8,128)S(1)}, u32[]{:S(2)}, u32[]{:S(2)}) collective-permute-start(f32[192,128]{1,0:T(8,128)S(1)} %collective-permute-done.16.refs_1_), channel_id=1, source_target_pairs={{0,8},{8,0},{16,24},{24,16},{32,40},{40,32},{48,56},{56,48},{64,72... | collective-permute-start | bytes 294920 | tf_op jit(solution)/shard_map/ppermute | solution.py:442
  102.4 16.3 %all-to-all-start = ((f32[8,8,128]{2,1,0:T(8,128)}), f32[8,8,128]{2,1,0:T(8,128)S(1)}, u32[]{:S(2)}, u32[]{:S(2)}) async-start(f32[8,8,128]{2,1,0:T(8,128)} %get-tuple-element.61), calls=%async_computation | async-start | bytes 65536 | tf_op jit(solution)/shard_map/all_to_all | solution.py:450
  (4 other events, 24.9 us)
where the time goes:
time: 120 us; the launch traced here: 119 us
  starting transfers between devices  52 us (43%)
  waiting for transfers between devices  35 us (29%)
  Pallas kernels  29.8 us (25%)
  local copies, waits for them, and re-layouts  1.82 us (2%)
    pallas_call x11, Pallas kernels, run(): pl.pallas_call(body, out_shape=out_shape, in_specs=[SMEM if a.dtype == jn...  29.8 us
    ppermute x6, waiting for transfers between devices, on_device(): lax.ppermute(sends[k], 'fac', ring_x(k))  9.77 us
    ppermute x6, starting transfers between devices, on_device(): lax.ppermute(sends[k], 'fac', ring_x(k))  9.07 us
    ppermute x4, starting transfers between devices, on_device(): others = [lax.ppermute(q, 'space', swap) for q in mine]  8.13 us
    ppermute x1, starting transfers between devices, on_device(): got = lax.ppermute(give, 'fac', ends)  7.83 us
    all_to_all x1, waiting for transfers between devices, on_device(): every = lax.all_to_all(total, 'fac', 0, 0, tiled=True)  7.76 us
    ppermute x3, waiting for transfers between devices, on_device(): over_z = [lax.ppermute(mine, 'space', ring_z(k)) for k in (1, 2, 3)]  7.4 us
    all_to_all x1, starting transfers between devices, on_device(): every = lax.all_to_all(total, 'fac', 0, 0, tiled=True)  7.24 us
  transfers between devices with their start and end apart: 24, of which 11 were waited for; matrix products, arithmetic and copies ran while one was open for 0% of the time, Pallas kernels for 3%

commit v1 on v0

--- a/solution.py
+++ b/solution.py
@@ -15,7 +15,6 @@
 BF16 = jnp.bfloat16
 HI = lax.Precision.HIGHEST
 VMEM = pl.BlockSpec(memory_space=pltpu.VMEM)
-PARAMS = pltpu.CompilerParams(vmem_limit_bytes=48 * 1024 * 1024)
 
 ORDER = 432
 EDGES = (0, 128, 256, 384)
@@ -31,7 +30,7 @@
 ANY = pl.BlockSpec(memory_space=pl.ANY)
 
 
-def call(body, out_shape, scratch=(), name=None, spec=VMEM):
+def call(body, out_shape, scratch=(), name=None, spec=VMEM, grant=48):
     def run(*args):
         return pl.pallas_call(
             body,
@@ -39,7 +38,7 @@
             in_specs=[SMEM if a.dtype == jnp.int32 else spec for a in args],
             out_specs=jax.tree.map(lambda _: VMEM, out_shape),
             scratch_shapes=list(scratch),
-            compiler_params=PARAMS,
+            compiler_params=pltpu.CompilerParams(vmem_limit_bytes=grant * 1024 * 1024),
             name=name,
         )(*args)
 
@@ -145,12 +144,17 @@
                 for a in (-1, 0, 1):
                     tap = 9 * (a + 1) + 3 * (b + 1) + (c + 1)
                     at = (1 + a) * 256
-                    x_ref[tap * 16 : (tap + 1) * 16, cols] = moved[:, at : at + 512]
-        x_ref[ORDER:, cols] = parts[s][16:, :]
-    for edge, start in zip(EDGES, STARTS):
-        tile = nt(x_ref[edge:ORDER, :], x_ref[edge : edge + 128, :])
-        out_ref[start : start + ORDER - edge, :] = tile
-    out_ref[GRAD_AT : GRAD_AT + ORDER + 128, :] = nt(x_ref[...], x_ref[ORDER:, :])
+                    x_ref[128 + tap * 16 : 144 + tap * 16, cols] = moved[:, at : at + 512]
+        x_ref[0:128, cols] = parts[s][16:, :]
+    wide = nt(x_ref[...], x_ref[0:256, :])
+    out_ref[COT_AT : COT_AT + 128, :] = wide[:128, :128]
+    out_ref[GRAD_AT : GRAD_AT + ORDER, :] = wide[128:, :128]
+    out_ref[STARTS[0] : STARTS[0] + ORDER, :] = wide[128:, 128:]
+    wide = nt(x_ref[256:, :], x_ref[256:512, :])
+    out_ref[STARTS[1] : STARTS[1] + ORDER - 128, :] = wide[:, :128]
+    out_ref[STARTS[2] : STARTS[2] + ORDER - 256, :] = wide[128:, 128:]
+    out_ref[STARTS[3] : STARTS[3] + ORDER - 384, :] = jnp.zeros((ORDER - 384, 128), F32)
+    out_ref[STARTS[3] : STARTS[3] + ORDER - 384, 0 : ORDER - 384] = nt(x_ref[512:, :], x_ref[512:, :])
     out_ref[COT_AT + 128 :, :] = jnp.zeros((PACKED - COT_AT - 128, 128), F32)
     for k in range(4):
         for half, ref in ((core, keep_ref), (1 - core, give_ref)):
@@ -405,6 +409,7 @@
         scratch=[pltpu.VMEM((512, 128), BF16)] * 2 + [pltpu.VMEM((128, 512), BF16), pltpu.SemaphoreType.DMA((2,))],
         name="prep",
         spec=ANY,
+        grant=60,
     )(place, act, cot)
     got = lax.ppermute(give, "fac", ends)
     own = [sends[0]] + [lax.ppermute(sends[k], "fac", ring_x(k)) for k in (1, 2, 3)]

time: 120 us -> 119 us (level)
  local copies, waits for them, and re-layouts: 1.82 us -> 0.02 us
    unnamed x8, local copies, waits for them, and re-layouts: 1.82 us -> 0.02 us
where the time goes in v1:
time: 119 us; the launch traced here: 118 us
  starting transfers between devices  51.8 us (44%)
  waiting for transfers between devices  35.2 us (30%)
  Pallas kernels  30 us (25%)
    pallas_call x11, Pallas kernels, run(): pl.pallas_call(body, out_shape=out_shape, in_specs=[SMEM if a.dtype == jn...  30 us
    ppermute x6, waiting for transfers between devices, on_device(): lax.ppermute(sends[k], 'fac', ring_x(k))  9.98 us
    ppermute x6, starting transfers between devices, on_device(): lax.ppermute(sends[k], 'fac', ring_x(k))  9.07 us
    ppermute x4, starting transfers between devices, on_device(): others = [lax.ppermute(q, 'space', swap) for q in mine]  8.13 us
    ppermute x1, starting transfers between devices, on_device(): got = lax.ppermute(give, 'fac', ends)  7.83 us
    all_to_all x1, waiting for transfers between devices, on_device(): every = lax.all_to_all(total, 'fac', 0, 0, tiled=True)  7.76 us
    ppermute x3, waiting for transfers between devices, on_device(): over_z = [lax.ppermute(mine, 'space', ring_z(k)) for k in (1, 2, 3)]  7.4 us
    all_to_all x1, starting transfers between devices, on_device(): every = lax.all_to_all(total, 'fac', 0, 0, tiled=True)  7.24 us
  transfers between devices with their start and end apart: 24, of which 11 were waited for; matrix products, arithmetic and copies ran while one was open for 0% of the time, Pallas kernels for 3%

profile of v1, /device:TPU:1, one launch (start us, length us, event | category | flops | bytes accessed | tf_op | source)
XLA Modules:
  0.0 118.4 jit_solution(2944619620933912144)
XLA Ops:
  1.3 2.7 %prep.1 = (bf16[192,512]{1,0:T(8,128)(2,1)}, bf16[144,512]{1,0:T(8,128)(2,1)}, bf16[144,512]{1,0:T(8,128)(2,1)}, bf16[144,512]{1,0:T(8,128)(2,1)}, bf16[144,512]{1,0:T(8,128)(2,1)}) custom-call(s32[4]{0:T(128)} %pad_add_fusion.place_ref, bf16[512,128]{1,0:T(8,128)(2,1)} %bitcast.11, bf16[512,128]{1,0:T(8,128)(2,1)} %bitcast.8), custom_call_target="tpu_custom_call" | custom-call | tf_op jit(solution)/shard_map/prep/pallas_call | solution.py:35
  4.0 7.8 %collective-permute-start = (bf16[192,512]{1,0:T(8,128)(2,1)}, bf16[192,512]{1,0:T(8,128)(2,1)S(1)}, u32[]{:S(2)}, u32[]{:S(2)}) collective-permute-start(bf16[192,512]{1,0:T(8,128)(2,1)} %get-tuple-element.32), channel_id=1, source_target_pairs={{0,4},{1,5},{2,6},{3,7},{4,0},{5,1},{6,2},{7,3},{8,12},{9,13},{10,... | collective-permute-start | bytes 589832 | tf_op jit(solution)/shard_map/ppermute | solution.py:414
  13.0 2.5 %collective-permute-start.2 = (bf16[144,512]{1,0:T(8,128)(2,1)}, bf16[144,512]{1,0:T(8,128)(2,1)S(1)}, u32[]{:S(2)}, u32[]{:S(2)}) collective-permute-start(bf16[144,512]{1,0:T(8,128)(2,1)} %get-tuple-element.35), channel_id=1, source_target_pairs={{0,2},{1,3},{2,0},{3,1},{4,6},{5,7},{6,4},{7,5},{8,10},{9,11},{10,... | collective-permute-start | bytes 442376 | tf_op jit(solution)/shard_map/ppermute | solution.py:415
  17.6 4.1 %collective-permute-done.2.refs_2_ = bf16[144,512]{1,0:T(8,128)(2,1)S(1)} collective-permute-done((bf16[144,512]{1,0:T(8,128)(2,1)}, bf16[144,512]{1,0:T(8,128)(2,1)S(1)}, u32[]{:S(2)}, u32[]{:S(2)}) %collective-permute-start.2) | collective-permute-done | bytes 147488 | tf_op jit(solution)/shard_map/ppermute | solution.py:415
  21.8 1.8 %collective-permute-start.4 = (bf16[144,512]{1,0:T(8,128)(2,1)S(1)}, bf16[144,512]{1,0:T(8,128)(2,1)S(1)}, u32[]{:S(2)}, u32[]{:S(2)}) collective-permute-start(bf16[144,512]{1,0:T(8,128)(2,1)S(1)} %get-tuple-element.43), channel_id=1, source_target_pairs={{0,1},{1,2},{2,3},{3,0},{4,5},{5,6},{6,7},{7,4},{8,9},{9,10},{10,1... | collective-permute-start | bytes 442376 | tf_op jit(solution)/shard_map/ppermute | solution.py:419
  23.6 2.0 %collective-permute-start.5 = (bf16[144,512]{1,0:T(8,128)(2,1)S(1)}, bf16[144,512]{1,0:T(8,128)(2,1)S(1)}, u32[]{:S(2)}, u32[]{:S(2)}) collective-permute-start(bf16[144,512]{1,0:T(8,128)(2,1)S(1)} %get-tuple-element.44), channel_id=1, source_target_pairs={{0,2},{1,3},{2,0},{3,1},{4,6},{5,7},{6,4},{7,5},{8,10},{9,11},{10,... | collective-permute-start | bytes 442376 | tf_op jit(solution)/shard_map/ppermute | solution.py:419
  27.1 3.8 %collective-permute-done.5.refs_6_ = bf16[144,512]{1,0:T(8,128)(2,1)S(1)} collective-permute-done((bf16[144,512]{1,0:T(8,128)(2,1)S(1)}, bf16[144,512]{1,0:T(8,128)(2,1)S(1)}, u32[]{:S(2)}, u32[]{:S(2)}) %collective-permute-start.5) | collective-permute-done | bytes 147488 | tf_op jit(solution)/shard_map/ppermute | solution.py:419
  30.9 5.7 %collective-permute-start.7 = (bf16[256,256]{1,0:T(8,128)(2,1)S(1)}, bf16[256,256]{1,0:T(8,128)(2,1)S(1)}, u32[]{:S(2)}, u32[]{:S(2)}) collective-permute-start(bf16[256,256]{1,0:T(8,128)(2,1)S(1)} %get-tuple-element.46), channel_id=1, source_target_pairs={{0,8},{8,16},{16,24},{24,32},{32,40},{40,48},{48,56},{56,64},{64,7... | collective-permute-start | bytes 393224 | tf_op jit(solution)/shard_map/ppermute | solution.py:423
  36.7 2.1 %collective-permute-start.8 = (bf16[256,256]{1,0:T(8,128)(2,1)S(1)}, bf16[256,256]{1,0:T(8,128)(2,1)S(1)}, u32[]{:S(2)}, u32[]{:S(2)}) collective-permute-start(bf16[256,256]{1,0:T(8,128)(2,1)S(1)} %get-tuple-element.47), channel_id=1, source_target_pairs={{8,0},{16,8},{24,16},{32,24},{40,32},{48,40},{56,48},{64,56},{72,6... | collective-permute-start | bytes 393224 | tf_op jit(solution)/shard_map/ppermute | solution.py:424
  38.8 4.3 %collective-permute-done.8.next_ref = bf16[256,256]{1,0:T(8,128)(2,1)S(1)} collective-permute-done((bf16[256,256]{1,0:T(8,128)(2,1)S(1)}, bf16[256,256]{1,0:T(8,128)(2,1)S(1)}, u32[]{:S(2)}, u32[]{:S(2)}) %collective-permute-start.8) | collective-permute-done | bytes 131104 | tf_op jit(solution)/shard_map/ppermute | solution.py:424
  43.1 2.9 %stats.1 = (f32[768,128]{1,0:T(8,128)S(1)}, f32[768,128]{1,0:T(8,128)S(1)}) custom-call(s32[4]{0:T(128)S(1)} %copy-done.3, bf16[256,256]{1,0:T(8,128)(2,1)S(1)} %collective-permute-done.7.prev_ref, bf16[256,256]{1,0:T(8,128)(2,1)S(1)} %collective-permute-done.8.next_ref, bf16[144,512]{1,0:T(8,128)(2,1)S(1)} %copy-done.1, ...), custom_call_target="tpu_custom_call" | custom-call | tf_op jit(solution)/shard_map/stats/pallas_call | solution.py:35
  46.1 1.7 %collective-permute-done.9.got_ref = f32[768,128]{1,0:T(8,128)S(1)} collective-permute-done((f32[768,128]{1,0:T(8,128)S(1)}, f32[768,128]{1,0:T(8,128)S(1)}, u32[]{:S(2)}, u32[]{:S(2)}) %collective-permute-start.9) | collective-permute-done | bytes 393248 | tf_op jit(solution)/shard_map/ppermute | solution.py:439
  49.3 3.8 %collective-permute-start.11 = (f32[192,128]{1,0:T(8,128)S(1)}, f32[192,128]{1,0:T(8,128)S(1)}, u32[]{:S(2)}, u32[]{:S(2)}) collective-permute-start(f32[192,128]{1,0:T(8,128)S(1)} %get-tuple-element.51), channel_id=1, source_target_pairs={{0,32},{8,40},{16,48},{24,56},{32,0},{40,8},{48,16},{56,24},{64,96... | collective-permute-start | bytes 294920 | tf_op jit(solution)/shard_map/ppermute | solution.py:441
  53.1 1.9 %in_grad.1 = bf16[512,128]{1,0:T(8,128)(2,1)} custom-call(bf16[256,256]{1,0:T(8,128)(2,1)S(1)} %collective-permute-done.7.prev_ref, bf16[512,128]{1,0:T(8,128)(2,1)S(1)} %bitcast.9, bf16[256,256]{1,0:T(8,128)(2,1)S(1)} %collective-permute-done.8.next_ref, bf16[27,128,128]{2,1,0:T(8,128)(2,1)S(1)} %copy-done), custom_call_target="tpu_custom_call" | custom-call | tf_op jit(solution)/shard_map/in_grad/pallas_call | solution.py:35
  55.0 3.0 %collective-permute-done.11.refs_2_ = f32[192,128]{1,0:T(8,128)S(1)} collective-permute-done((f32[192,128]{1,0:T(8,128)S(1)}, f32[192,128]{1,0:T(8,128)S(1)}, u32[]{:S(2)}, u32[]{:S(2)}) %collective-permute-start.11) | collective-permute-done | bytes 98336 | tf_op jit(solution)/shard_map/ppermute | solution.py:441
  58.1 1.9 %collective-permute-start.14 = (f32[192,128]{1,0:T(8,128)S(1)}, f32[192,128]{1,0:T(8,128)S(1)}, u32[]{:S(2)}, u32[]{:S(2)}) collective-permute-start(f32[192,128]{1,0:T(8,128)S(1)} %fold_y.1.a_ref), channel_id=1, source_target_pairs={{0,128},{8,136},{16,144},{24,152},{32,160},{40,168},{48,176},{56,1... | collective-permute-start | bytes 294920 | tf_op jit(solution)/shard_map/ppermute | solution.py:444
  61.6 6.6 %collective-permute-done.14.c_ref = f32[192,128]{1,0:T(8,128)S(1)} collective-permute-done((f32[192,128]{1,0:T(8,128)S(1)}, f32[192,128]{1,0:T(8,128)S(1)}, u32[]{:S(2)}, u32[]{:S(2)}) %collective-permute-start.14) | collective-permute-done | bytes 98336 | tf_op jit(solution)/shard_map/ppermute | solution.py:444
  68.2 3.0 %collective-permute-start.18 = (f32[192,128]{1,0:T(8,128)S(1)}, f32[192,128]{1,0:T(8,128)S(1)}, u32[]{:S(2)}, u32[]{:S(2)}) collective-permute-start(f32[192,128]{1,0:T(8,128)S(1)} %fold_z.1.refs_0_), channel_id=1, source_target_pairs={{0,48},{8,56},{16,0},{24,8},{32,16},{40,24},{48,32},{56,40},{64,11... | collective-permute-start | bytes 294920 | tf_op jit(solution)/shard_map/ppermute | solution.py:446
  71.9 1.9 %collective-permute-start.19 = (f32[192,128]{1,0:T(8,128)S(1)}, f32[192,128]{1,0:T(8,128)S(1)}, u32[]{:S(2)}, u32[]{:S(2)}) collective-permute-start(f32[192,128]{1,0:T(8,128)S(1)} %fold_z.1.refs_0_), channel_id=1, source_target_pairs={{0,8},{8,0},{16,24},{24,16},{32,40},{40,32},{48,56},{56,48},{64,72... | collective-permute-start | bytes 294920 | tf_op jit(solution)/shard_map/ppermute | solution.py:447
  73.8 2.6 %collective-permute-start.22 = (f32[192,128]{1,0:T(8,128)S(1)}, f32[192,128]{1,0:T(8,128)S(1)}, u32[]{:S(2)}, u32[]{:S(2)}) collective-permute-start(f32[192,128]{1,0:T(8,128)S(1)} %collective-permute-done.18.refs_3_), channel_id=1, source_target_pairs={{0,8},{8,0},{16,24},{24,16},{32,40},{40,32},{48,56},{56,48},{64,72... | collective-permute-start | bytes 294920 | tf_op jit(solution)/shard_map/ppermute | solution.py:447
  76.4 2.7 %collective-permute-start.21 = (f32[192,128]{1,0:T(8,128)S(1)}, f32[192,128]{1,0:T(8,128)S(1)}, u32[]{:S(2)}, u32[]{:S(2)}) collective-permute-start(f32[192,128]{1,0:T(8,128)S(1)} %collective-permute-done.17.refs_2_), channel_id=1, source_target_pairs={{0,8},{8,0},{16,24},{24,16},{32,40},{40,32},{48,56},{56,48},{64,72... | collective-permute-start | bytes 294920 | tf_op jit(solution)/shard_map/ppermute | solution.py:447
  81.0 20.5 %forward.1 = (f32[432,128]{1,0:T(8,128)S(1)}, f32[960,128]{1,0:T(8,128)S(1)}, f32[128,128]{1,0:T(8,128)S(1)}, f32[8,8,128]{2,1,0:T(8,128)}) custom-call(s32[4]{0:T(128)S(1)} %copy-done.3, f32[192,128]{1,0:T(8,128)S(1)} %fold_z.1.refs_0_, f32[192,128]{1,0:T(8,128)S(1)} %collective-permute-done.16.refs_1_, f32[192,128]{1,0:T(8,128)S(1)} %collective-permute-done.17.refs_2_, ...), custom_call_target="tpu_custom_call" | custom-call | tf_op jit(solution)/shard_map/forward/pallas_call | solution.py:35
  101.4 7.2 %all-to-all-start = ((f32[8,8,128]{2,1,0:T(8,128)}), f32[8,8,128]{2,1,0:T(8,128)S(1)}, u32[]{:S(2)}, u32[]{:S(2)}) async-start(f32[8,8,128]{2,1,0:T(8,128)} %get-tuple-element.61), calls=%async_computation | async-start | bytes 65536 | tf_op jit(solution)/shard_map/all_to_all | solution.py:455
  109.9 7.8 %all-to-all-done.parts_ref = f32[8,8,128]{2,1,0:T(8,128)S(1)} async-done(((f32[8,8,128]{2,1,0:T(8,128)}), f32[8,8,128]{2,1,0:T(8,128)S(1)}, u32[]{:S(2)}, u32[]{:S(2)}) %all-to-all-start) | async-done | bytes 32800 | tf_op jit(solution)/shard_map/all_to_all | solution.py:455
  (44 shorter events, 13.3 us)
Async XLA Ops:
  4.0 17.8 %collective-permute-start = (bf16[192,512]{1,0:T(8,128)(2,1)}, bf16[192,512]{1,0:T(8,128)(2,1)S(1)}, u32[]{:S(2)}, u32[]{:S(2)}) collective-permute-start(bf16[192,512]{1,0:T(8,128)(2,1)} %get-tuple-element.32), channel_id=1, source_target_pairs={{0,4},{1,5},{2,6},{3,7},{4,0},{5,1},{6,2},{7,3},{8,12},{9,13},{10,... | collective-permute-start | bytes 589832 | tf_op jit(solution)/shard_map/ppermute | solution.py:414
  11.8 5.8 %collective-permute-start.1 = (bf16[144,512]{1,0:T(8,128)(2,1)}, bf16[144,512]{1,0:T(8,128)(2,1)S(1)}, u32[]{:S(2)}, u32[]{:S(2)}) collective-permute-start(bf16[144,512]{1,0:T(8,128)(2,1)} %get-tuple-element.34), channel_id=1, source_target_pairs={{0,1},{1,2},{2,3},{3,0},{4,5},{5,6},{6,7},{7,4},{8,9},{9,10},{10,1... | collective-permute-start | bytes 442376 | tf_op jit(solution)/shard_map/ppermute | solution.py:415
  13.0 8.8 %collective-permute-start.2 = (bf16[144,512]{1,0:T(8,128)(2,1)}, bf16[144,512]{1,0:T(8,128)(2,1)S(1)}, u32[]{:S(2)}, u32[]{:S(2)}) collective-permute-start(bf16[144,512]{1,0:T(8,128)(2,1)} %get-tuple-element.35), channel_id=1, source_target_pairs={{0,2},{1,3},{2,0},{3,1},{4,6},{5,7},{6,4},{7,5},{8,10},{9,11},{10,... | collective-permute-start | bytes 442376 | tf_op jit(solution)/shard_map/ppermute | solution.py:415
  15.5 6.3 %collective-permute-start.3 = (bf16[144,512]{1,0:T(8,128)(2,1)}, bf16[144,512]{1,0:T(8,128)(2,1)S(1)}, u32[]{:S(2)}, u32[]{:S(2)}) collective-permute-start(bf16[144,512]{1,0:T(8,128)(2,1)} %get-tuple-element.36), channel_id=1, source_target_pairs={{0,3},{1,0},{2,1},{3,2},{4,7},{5,4},{6,5},{7,6},{8,11},{9,8},{10,9... | collective-permute-start | bytes 442376 | tf_op jit(solution)/shard_map/ppermute | solution.py:415
  21.8 5.3 %collective-permute-start.4 = (bf16[144,512]{1,0:T(8,128)(2,1)S(1)}, bf16[144,512]{1,0:T(8,128)(2,1)S(1)}, u32[]{:S(2)}, u32[]{:S(2)}) collective-permute-start(bf16[144,512]{1,0:T(8,128)(2,1)S(1)} %get-tuple-element.43), channel_id=1, source_target_pairs={{0,1},{1,2},{2,3},{3,0},{4,5},{5,6},{6,7},{7,4},{8,9},{9,10},{10,1... | collective-permute-start | bytes 442376 | tf_op jit(solution)/shard_map/ppermute | solution.py:419
  23.6 7.3 %collective-permute-start.5 = (bf16[144,512]{1,0:T(8,128)(2,1)S(1)}, bf16[144,512]{1,0:T(8,128)(2,1)S(1)}, u32[]{:S(2)}, u32[]{:S(2)}) collective-permute-start(bf16[144,512]{1,0:T(8,128)(2,1)S(1)} %get-tuple-element.44), channel_id=1, source_target_pairs={{0,2},{1,3},{2,0},{3,1},{4,6},{5,7},{6,4},{7,5},{8,10},{9,11},{10,... | collective-permute-start | bytes 442376 | tf_op jit(solution)/shard_map/ppermute | solution.py:419
  25.6 5.3 %collective-permute-start.6 = (bf16[144,512]{1,0:T(8,128)(2,1)S(1)}, bf16[144,512]{1,0:T(8,128)(2,1)S(1)}, u32[]{:S(2)}, u32[]{:S(2)}) collective-permute-start(bf16[144,512]{1,0:T(8,128)(2,1)S(1)} %get-tuple-element.45), channel_id=1, source_target_pairs={{0,3},{1,0},{2,1},{3,2},{4,7},{5,4},{6,5},{7,6},{8,11},{9,8},{10,9... | collective-permute-start | bytes 442376 | tf_op jit(solution)/shard_map/ppermute | solution.py:419
  30.9 7.8 %collective-permute-start.7 = (bf16[256,256]{1,0:T(8,128)(2,1)S(1)}, bf16[256,256]{1,0:T(8,128)(2,1)S(1)}, u32[]{:S(2)}, u32[]{:S(2)}) collective-permute-start(bf16[256,256]{1,0:T(8,128)(2,1)S(1)} %get-tuple-element.46), channel_id=1, source_target_pairs={{0,8},{8,16},{16,24},{24,32},{32,40},{40,48},{48,56},{56,64},{64,7... | collective-permute-start | bytes 393224 | tf_op jit(solution)/shard_map/ppermute | solution.py:423
  36.7 6.4 %collective-permute-start.8 = (bf16[256,256]{1,0:T(8,128)(2,1)S(1)}, bf16[256,256]{1,0:T(8,128)(2,1)S(1)}, u32[]{:S(2)}, u32[]{:S(2)}) collective-permute-start(bf16[256,256]{1,0:T(8,128)(2,1)S(1)} %get-tuple-element.47), channel_id=1, source_target_pairs={{8,0},{16,8},{24,16},{32,24},{40,32},{48,40},{56,48},{64,56},{72,6... | collective-permute-start | bytes 393224 | tf_op jit(solution)/shard_map/ppermute | solution.py:424
  46.0 1.8 %collective-permute-start.9 = (f32[768,128]{1,0:T(8,128)S(1)}, f32[768,128]{1,0:T(8,128)S(1)}, u32[]{:S(2)}, u32[]{:S(2)}) collective-permute-start(f32[768,128]{1,0:T(8,128)S(1)} %get-tuple-element.49), channel_id=1, source_target_pairs={{0,8},{8,0},{16,24},{24,16},{32,40},{40,32},{48,56},{56,48},{64,72... | collective-permute-start | bytes 1179656 | tf_op jit(solution)/shard_map/ppermute | solution.py:439
  47.9 7.1 %collective-permute-start.10 = (f32[192,128]{1,0:T(8,128)S(1)}, f32[192,128]{1,0:T(8,128)S(1)}, u32[]{:S(2)}, u32[]{:S(2)}) collective-permute-start(f32[192,128]{1,0:T(8,128)S(1)} %get-tuple-element.50), channel_id=1, source_target_pairs={{0,16},{8,24},{16,32},{24,40},{32,48},{40,56},{48,0},{56,8},{64,80... | collective-permute-start | bytes 294920 | tf_op jit(solution)/shard_map/ppermute | solution.py:441
  49.3 8.7 %collective-permute-start.11 = (f32[192,128]{1,0:T(8,128)S(1)}, f32[192,128]{1,0:T(8,128)S(1)}, u32[]{:S(2)}, u32[]{:S(2)}) collective-permute-start(f32[192,128]{1,0:T(8,128)S(1)} %get-tuple-element.51), channel_id=1, source_target_pairs={{0,32},{8,40},{16,48},{24,56},{32,0},{40,8},{48,16},{56,24},{64,96... | collective-permute-start | bytes 294920 | tf_op jit(solution)/shard_map/ppermute | solution.py:441
  53.1 4.9 %collective-permute-start.12 = (f32[192,128]{1,0:T(8,128)S(1)}, f32[192,128]{1,0:T(8,128)S(1)}, u32[]{:S(2)}, u32[]{:S(2)}) collective-permute-start(f32[192,128]{1,0:T(8,128)S(1)} %get-tuple-element.52), channel_id=1, source_target_pairs={{0,48},{8,56},{16,0},{24,8},{32,16},{40,24},{48,32},{56,40},{64,11... | collective-permute-start | bytes 294920 | tf_op jit(solution)/shard_map/ppermute | solution.py:441
  58.0 3.5 %collective-permute-start.15 = (f32[192,128]{1,0:T(8,128)S(1)}, f32[192,128]{1,0:T(8,128)S(1)}, u32[]{:S(2)}, u32[]{:S(2)}) collective-permute-start(f32[192,128]{1,0:T(8,128)S(1)} %fold_y.1.a_ref), channel_id=1, source_target_pairs={{0,192},{8,200},{16,208},{24,216},{32,224},{40,232},{48,240},{56,2... | collective-permute-start | bytes 294920 | tf_op jit(solution)/shard_map/ppermute | solution.py:444
  58.1 10.0 %collective-permute-start.14 = (f32[192,128]{1,0:T(8,128)S(1)}, f32[192,128]{1,0:T(8,128)S(1)}, u32[]{:S(2)}, u32[]{:S(2)}) collective-permute-start(f32[192,128]{1,0:T(8,128)S(1)} %fold_y.1.a_ref), channel_id=1, source_target_pairs={{0,128},{8,136},{16,144},{24,152},{32,160},{40,168},{48,176},{56,1... | collective-permute-start | bytes 294920 | tf_op jit(solution)/shard_map/ppermute | solution.py:444
  60.0 8.1 %collective-permute-start.13 = (f32[192,128]{1,0:T(8,128)S(1)}, f32[192,128]{1,0:T(8,128)S(1)}, u32[]{:S(2)}, u32[]{:S(2)}) collective-permute-start(f32[192,128]{1,0:T(8,128)S(1)} %fold_y.1.a_ref), channel_id=1, source_target_pairs={{0,64},{8,72},{16,80},{24,88},{32,96},{40,104},{48,112},{56,120},{... | collective-permute-start | bytes 294920 | tf_op jit(solution)/shard_map/ppermute | solution.py:444
  68.2 5.6 %collective-permute-start.18 = (f32[192,128]{1,0:T(8,128)S(1)}, f32[192,128]{1,0:T(8,128)S(1)}, u32[]{:S(2)}, u32[]{:S(2)}) collective-permute-start(f32[192,128]{1,0:T(8,128)S(1)} %fold_z.1.refs_0_), channel_id=1, source_target_pairs={{0,48},{8,56},{16,0},{24,8},{32,16},{40,24},{48,32},{56,40},{64,11... | collective-permute-start | bytes 294920 | tf_op jit(solution)/shard_map/ppermute | solution.py:446
  71.2 5.2 %collective-permute-start.17 = (f32[192,128]{1,0:T(8,128)S(1)}, f32[192,128]{1,0:T(8,128)S(1)}, u32[]{:S(2)}, u32[]{:S(2)}) collective-permute-start(f32[192,128]{1,0:T(8,128)S(1)} %fold_z.1.refs_0_), channel_id=1, source_target_pairs={{0,32},{8,40},{16,48},{24,56},{32,0},{40,8},{48,16},{56,24},{64,96... | collective-permute-start | bytes 294920 | tf_op jit(solution)/shard_map/ppermute | solution.py:446
  71.7 7.3 %collective-permute-start.16 = (f32[192,128]{1,0:T(8,128)S(1)}, f32[192,128]{1,0:T(8,128)S(1)}, u32[]{:S(2)}, u32[]{:S(2)}) collective-permute-start(f32[192,128]{1,0:T(8,128)S(1)} %fold_z.1.refs_0_), channel_id=1, source_target_pairs={{0,16},{8,24},{16,32},{24,40},{32,48},{40,56},{48,0},{56,8},{64,80... | collective-permute-start | bytes 294920 | tf_op jit(solution)/shard_map/ppermute | solution.py:446
  71.9 8.1 %collective-permute-start.19 = (f32[192,128]{1,0:T(8,128)S(1)}, f32[192,128]{1,0:T(8,128)S(1)}, u32[]{:S(2)}, u32[]{:S(2)}) collective-permute-start(f32[192,128]{1,0:T(8,128)S(1)} %fold_z.1.refs_0_), channel_id=1, source_target_pairs={{0,8},{8,0},{16,24},{24,16},{32,40},{40,32},{48,56},{56,48},{64,72... | collective-permute-start | bytes 294920 | tf_op jit(solution)/shard_map/ppermute | solution.py:447
  73.8 6.3 %collective-permute-start.22 = (f32[192,128]{1,0:T(8,128)S(1)}, f32[192,128]{1,0:T(8,128)S(1)}, u32[]{:S(2)}, u32[]{:S(2)}) collective-permute-start(f32[192,128]{1,0:T(8,128)S(1)} %collective-permute-done.18.refs_3_), channel_id=1, source_target_pairs={{0,8},{8,0},{16,24},{24,16},{32,40},{40,32},{48,56},{56,48},{64,72... | collective-permute-start | bytes 294920 | tf_op jit(solution)/shard_map/ppermute | solution.py:447
  76.4 3.7 %collective-permute-start.21 = (f32[192,128]{1,0:T(8,128)S(1)}, f32[192,128]{1,0:T(8,128)S(1)}, u32[]{:S(2)}, u32[]{:S(2)}) collective-permute-start(f32[192,128]{1,0:T(8,128)S(1)} %collective-permute-done.17.refs_2_), channel_id=1, source_target_pairs={{0,8},{8,0},{16,24},{24,16},{32,40},{40,32},{48,56},{56,48},{64,72... | collective-permute-start | bytes 294920 | tf_op jit(solution)/shard_map/ppermute | solution.py:447
  79.0 1.9 %collective-permute-start.20 = (f32[192,128]{1,0:T(8,128)S(1)}, f32[192,128]{1,0:T(8,128)S(1)}, u32[]{:S(2)}, u32[]{:S(2)}) collective-permute-start(f32[192,128]{1,0:T(8,128)S(1)} %collective-permute-done.16.refs_1_), channel_id=1, source_target_pairs={{0,8},{8,0},{16,24},{24,16},{32,40},{40,32},{48,56},{56,48},{64,72... | collective-permute-start | bytes 294920 | tf_op jit(solution)/shard_map/ppermute | solution.py:447
  101.4 16.3 %all-to-all-start = ((f32[8,8,128]{2,1,0:T(8,128)}), f32[8,8,128]{2,1,0:T(8,128)S(1)}, u32[]{:S(2)}, u32[]{:S(2)}) async-start(f32[8,8,128]{2,1,0:T(8,128)} %get-tuple-element.61), calls=%async_computation | async-start | bytes 65536 | tf_op jit(solution)/shard_map/all_to_all | solution.py:455
  (4 other events, 60.8 us)
